TPU v7x, 256 devices: a whole 4x4x8 slice. The times are simulated.
256 devices in a mesh: chan: 64 (over x, y_lo, z), win: 4 (over y_hi, core).
Axes of the slice: x: 4, y: 4 (y_hi: 2, y_lo: 2; y = y_hi * 2 + y_lo), z: 8, core: 2. Of those that a mesh axis runs over, the one named last changes fastest.
Arguments:
- traces: bfloat16 [1024, 192, 1500], P('chan', 'win'), may hold values from -6 to 6
- source_index: int32 [64], replicated, may hold values from 0 to 1023
Outputs:
- stack: float32 [2, 64, 1024, 256], P(None, 'win', 'chan')
All inputs are finite; a program needn't handle non-finite values.
Results may differ from a plain program's by a relative error of at most 0.0058.
Values may be sent and summed in bfloat16 or wider, within the bound.
A program may use at most 64 MiB of HBM per device.

v0:
```python
import math

import jax
import jax.numpy as jnp
from jax import lax
from jax.sharding import PartitionSpec as P

F = 256
F0 = 1
K = 64
GAUGE = 4


def shifted(block, axis, distance):
    devices = range(lax.axis_size(axis))
    route = [(i - distance, i) for i in devices if i - distance in devices]
    return lax.ppermute(block, axis, route)


def make_table(length, nbins):
    times = jnp.arange(length, dtype=jnp.int32)[:, None]
    bins = jnp.arange(nbins, dtype=jnp.int32)[None, :] + F0
    phase = (times * bins % length).astype(jnp.float32) * (2.0 * math.pi / length)
    return jnp.concatenate([jnp.cos(phase), -jnp.sin(phase)], axis=1).astype(jnp.bfloat16)


def per_device(traces, source_index):
    chans, wins, length = traces.shape
    nbins = F
    upper = shifted(traces[:GAUGE], "chan", -1)
    ext = jnp.concatenate([traces, upper], axis=0).astype(jnp.float32)
    diff = ext[GAUGE:] - ext[:-GAUGE]
    scale = jnp.sqrt(jnp.mean(diff * diff, axis=2, keepdims=True) + 1e-05)
    normed = (diff / scale).astype(jnp.bfloat16).reshape(chans * wins, length)
    spec = jnp.dot(normed, make_table(length, nbins), preferred_element_type=jnp.float32)
    real_part = spec[:, :nbins]
    imag_part = spec[:, nbins:]
    rows = jnp.arange(nbins, dtype=jnp.int32)[:, None]
    cols = jnp.arange(nbins, dtype=jnp.int32)[None, :]
    band = (jnp.abs(rows - cols) <= K).astype(jnp.float32)
    counts = jnp.sum(band, axis=0)
    magnitude = jnp.sqrt(real_part * real_part + imag_part * imag_part)
    smooth = jnp.dot(magnitude, band, precision=lax.Precision.HIGHEST) / counts
    white_re = (real_part / (smooth + 1e-06)).astype(jnp.bfloat16).reshape(chans, wins, nbins)
    white_im = (imag_part / (smooth + 1e-06)).astype(jnp.bfloat16).reshape(chans, wins, nbins)
    first = lax.axis_index("chan") * chans
    local_ids = first + jnp.arange(chans, dtype=jnp.int32)
    picker = (source_index[:, None] == local_ids[None, :]).astype(jnp.bfloat16)
    picked = jnp.stack(
        [
            jnp.einsum("sc,cwf->swf", picker, white_re, preferred_element_type=jnp.float32),
            jnp.einsum("sc,cwf->swf", picker, white_im, preferred_element_type=jnp.float32),
        ]
    )
    sources = lax.psum(picked, "chan").astype(jnp.bfloat16)
    source_re = sources[0]
    source_im = sources[1]
    real_out = jnp.einsum(
        "swf,cwf->scf", source_re, white_re, preferred_element_type=jnp.float32
    ) + jnp.einsum("swf,cwf->scf", source_im, white_im, preferred_element_type=jnp.float32)
    imag_out = jnp.einsum(
        "swf,cwf->scf", source_im, white_re, preferred_element_type=jnp.float32
    ) - jnp.einsum("swf,cwf->scf", source_re, white_im, preferred_element_type=jnp.float32)
    total_windows = wins * lax.axis_size("win")
    terms = jnp.stack([real_out, imag_out]) * (1.0 / total_windows)
    return lax.psum_scatter(terms, "win", scatter_dimension=1, tiled=True)


def solution(mesh):
    return jax.shard_map(
        per_device,
        mesh=mesh,
        in_specs=(P("chan", "win", None), P()),
        out_specs=P(None, "win", "chan", None),
        check_vma=False,
    )
```

profile of v0, /device:TPU:1, one launch (start us, length us, event | category | flops | bytes accessed | tf_op | source)
XLA Modules:
  0.0 495.1 jit_solution(2853881477617804828)
XLA Ops:
  6.5 0.0 copy-start.6
  6.5 0.0 reduce-scatter.2.cloned.1.call-start
  6.5 1.3 slice.21
  7.8 1.3 collective-permute-start
  9.1 0.1 convert_reduce_fusion
  9.2 6.6 %cosine_convert_fusion = (bf16[1500,256]{1,0:T(8,128)(2,1)S(1)}, bf16[1500,256]{1,0:T(8,128)(2,1)S(1)}) fusion(s32[256]{0:T(256)S(1)} %iota_add_fusion), kind=kLoop, calls=%fused_computation.18 | loop fusion | flops 4608000 | bytes 1537024 | tf_op jit(solution)/shard_map/convert
  15.8 7.5 %collective-permute-done = bf16[4,48,1500]{2,1,0:T(8,128)(2,1)S(1)} collective-permute-done((bf16[4,48,1500]{2,1,0:T(8,128)(2,1)S(1)}, bf16[4,48,1500]{2,1,0:T(8,128)(2,1)S(1)}, u32[]{:S(2)}, u32[]{:S(2)}) %collective-permute-start) | collective-permute-done | bytes 576032 | tf_op jit(solution)/shard_map/ppermute | solution.py:17
  23.3 0.0 copy-done.6
  23.3 0.4 maximum_convert_fusion
  23.7 0.5 multiply_reduce_fusion
  24.2 0.9 divide_convert_fusion
  25.2 1.4 fusion.2
  26.5 0.0 copy-start.8
  26.5 0.8 divide_convert_fusion.1
  27.4 0.0 copy-start.7
  27.4 0.7 copy-done.7
  28.1 1.9 copy.42
  30.0 0.0 copy-done.8
  30.0 1.7 convolution_bitcast_fusion
  31.7 2.4 convolution_bitcast_fusion.1
  34.1 1.8 copy.40
  35.9 5.2 %pad_maximum_fusion = f32[2,64,48,256]{3,1,2,0:T(8,128)} fusion(f32[1,64,48,256]{3,1,2,0:T(8,128)S(1)} %convolution_bitcast_fusion, f32[1,64,48,256]{3,1,2,0:T(8,128)} %convolution_bitcast_fusion.1), kind=kLoop, calls=%fused_computation | loop fusion | flops 1572864 | bytes 12582912 | tf_op jit(solution)/shard_map/stack | solution.py:49
  41.1 319.4 %all-reduce.1 = bf16[2,64,48,256]{3,1,2,0:T(8,128)(2,1)S(1)} all-reduce(f32[2,64,48,256]{3,1,2,0:T(8,128)} %pad_maximum_fusion), channel_id=1, replica_groups=mesh['chan'=64,'win'=4] {'chan'}, use_global_device_ids=true, to_apply=%region_2.3 | all-reduce | flops 1572864 | bytes 9437184 | tf_op jit(solution)/shard_map/psum | solution.py:55
  360.5 1.9 slice_bitcast_fusion.1
  362.4 4.0 copy.43
  366.4 5.3 %copy.41 = bf16[64,48,256]{0,1,2:T(8,128)(2,1)} copy(bf16[64,48,256]{2,0,1:T(8,128)(2,1)} %get-tuple-element.5) | data formatting | bytes 3145728 | tf_op jit(solution)/shard_map/squeeze | solution.py:56
  371.7 0.0 copy-start
  371.7 0.0 copy-start.1
  371.7 3.6 fusion.30
  375.3 0.0 copy-done
  375.3 0.0 copy-done.1
  375.4 0.0 copy-start.2
  375.4 2.3 fusion.32
  377.6 0.0 copy-done.2
  377.6 2.3 fusion.29
  379.9 2.3 fusion.31
  382.2 2.9 copy.45
  385.1 0.0 copy-start.3
  385.1 3.9 copy.44
  389.0 0.0 copy-done.3
  389.0 2.3 copy.51
  391.3 0.0 copy-start.4
  391.3 0.0 copy-start.5
  391.4 3.9 copy.50
  395.3 0.0 copy-done.4
  395.3 0.0 copy-done.5
  395.3 1.7 subtract_bitcast_fusion
  397.0 0.2 maximum_multiply_fusion
  397.3 1.5 copy.52
  398.8 0.0 reduce-scatter.2.cloned.1.call-update
  398.8 87.6 %reduce-scatter.2.cloned.1.call-done = f32[2,16,16,256]{3,2,0,1:T(8,128)} async-done(((f32[2,64,16,256]{3,2,0,1:T(8,128)}), f32[2,16,16,256]{3,2,0,1:T(8,128)}) %reduce-scatter.2.cloned.1.call-update) | async-done | bytes 524304 | tf_op jit(solution)/shard_map/reduce_scatter | solution.py:66
  486.4 1.9 copy.53
  (3 shorter events, 0.0 us)
Async XLA Ops:
  6.5 16.8 %copy-start.6 = (bf16[16,48,1500]{2,1,0:T(8,128)(2,1)S(1)}, bf16[16,48,1500]{2,1,0:T(8,128)(2,1)}, u32[]{:S(2)}) copy-start(bf16[16,48,1500]{2,1,0:T(8,128)(2,1)} %param.2) | copy-start | bytes 6912004
  6.5 479.9 %reduce-scatter.2.cloned.1.call-start = ((), (), s32[]{:S(2)}) async-start(), calls=%async_computation.1 | async-start | bytes 2621440 | tf_op jit(solution)/shard_map/reduce_scatter | solution.py:66
  7.8 15.5 %collective-permute-start = (bf16[4,48,1500]{2,1,0:T(8,128)(2,1)S(1)}, bf16[4,48,1500]{2,1,0:T(8,128)(2,1)S(1)}, u32[]{:S(2)}, u32[]{:S(2)}) collective-permute-start(bf16[4,48,1500]{2,1,0:T(8,128)(2,1)S(1)} %slice.21), channel_id=1, source_target_pairs={{4,0},{8,4},{12,8},{16,12},{20,16},{24,20},{28,24},{32,28},{36,32}... | collective-permute-start | bytes 1728008 | tf_op jit(solution)/shard_map/ppermute | solution.py:17
  26.5 3.5 copy-start.8
  27.4 0.7 copy-start.7
  371.7 3.6 copy-start
  371.7 3.6 copy-start.1
  375.4 2.3 copy-start.2
  385.1 3.9 copy-start.3
  391.3 3.9 copy-start.4
  391.3 4.0 copy-start.5
Sparse Core Ops, SparseCore 0:
  398.9 87.4 reduce-scatter.1
where the time goes:
time: 496 us; the launch traced here: 495 us
  blocking collectives  319 us (64%)
  waiting for transfers between devices  95.1 us (19%)
  local copies, waits for them, and re-layouts  33.4 us (7%)
  matrix products  16.7 us (3%)
  other arithmetic  15.6 us (3%)
  between operations  13.5 us (3%)
    psum x1, blocking collectives, per_device(): sources = lax.psum(picked, 'chan').astype(jnp.bfloat16)  319 us
    reduce_scatter x1, waiting for transfers between devices, per_device(): return lax.psum_scatter(terms, 'win', scatter_dimension=1, tiled=True)  87.6 us
  transfers between devices with their start and end apart: 2, of which 2 were waited for; matrix products, arithmetic and copies ran while one was open for 1% of the time, Pallas kernels for 0%

commit v1 on v0

v1 whole, which is shorter than its diff:
```python
import functools
import math

import jax
import jax.numpy as jnp
import ml_dtypes
import numpy as np
from jax import lax
from jax.experimental import pallas as pl
from jax.experimental.pallas import tpu as pltpu
from jax.sharding import PartitionSpec as P

F = 256
F0 = 1
K = 64
GAUGE = 4
MESH = pl.DeviceIdType.MESH
BF16 = jnp.bfloat16
F32 = jnp.float32
NT = (((1,), (1,)), ((), ()))


def make_table(length):
    times = np.arange(length, dtype=np.int64)[None, :]
    bins = np.arange(F, dtype=np.int64)[:, None] + F0
    phase = (times * bins % length).astype(np.float32) * np.float32(2.0 * math.pi / length)
    phase = phase.astype(np.float64)
    return np.concatenate([np.cos(phase), -np.sin(phase)], axis=0).astype(np.float32).astype(ml_dtypes.bfloat16)


def make_band():
    rows = np.arange(F)[:, None]
    cols = np.arange(F)[None, :]
    return (np.abs(rows - cols) <= K).astype(ml_dtypes.bfloat16)


def body(n, sizes, index_ref, traces, table, band, out_ref, prev, nxt, norm_buf, mixed, sent, held, acc, core_out, core_in,
         y_out, y_in, back_out, back_in, back_f32, halves, halo_send, halo_recv, a2a_send, a2a_recv, core_send, core_recv,
         y_send, y_recv, back_send, back_recv):
    chans, wins, length, groups, parts = sizes
    side = GAUGE // 2
    gw = wins // groups
    me = lax.axis_index("chan")
    win = lax.axis_index("win")
    core_peer = win + 1 - 2 * lax.rem(win, 2)
    y_peer = lax.rem(win + 2, 4)
    right, left = lax.rem(me + 1, n), lax.rem(me + n - 1, n)

    barrier = pltpu.get_barrier_semaphore()

    def greet(d, carry):
        pl.semaphore_signal(barrier, inc=1, device_id={"chan": lax.rem(me + d, n)}, device_id_type=MESH)
        return carry

    lax.fori_loop(1, n, greet, 0)
    pl.semaphore_signal(barrier, inc=1, device_id={"win": core_peer}, device_id_type=MESH)
    pl.semaphore_signal(barrier, inc=1, device_id={"win": y_peer}, device_id_type=MESH)
    pl.semaphore_wait(barrier, n + 1)

    def halo(g, way):
        at = pl.ds(pl.multiple_of(g * gw, gw), gw)
        if way == 0:
            return pltpu.make_async_remote_copy(
                src_ref=traces.at[pl.ds(0, side), at], dst_ref=nxt.at[:, at], send_sem=halo_send.at[g, 0],
                recv_sem=halo_recv.at[g, 0], device_id={"chan": left}, device_id_type=MESH)
        return pltpu.make_async_remote_copy(
            src_ref=traces.at[pl.ds(chans - side, side), at], dst_ref=prev.at[:, at], send_sem=halo_send.at[g, 1],
            recv_sem=halo_recv.at[g, 1], device_id={"chan": right}, device_id_type=MESH)

    for g in range(groups):
        for way in range(2):
            halo(g, way).start()

    bins = lax.broadcasted_iota(jnp.int32, (F, 1), 0)
    counts = jnp.minimum(bins + K, F - 1) - jnp.maximum(bins - K, 0) + 1
    per_count = 1.0 / counts.astype(F32)
    lane = lax.broadcasted_iota(jnp.int32, (n, 128), 1)

    def whiten(g, carry):
        at = pl.ds(pl.multiple_of(g * gw, gw), gw)
        halo(g, 0).wait()
        halo(g, 1).wait()
        for i in range(chans):
            if i < side:
                low = prev[i, at, :].astype(F32)
            else:
                low = traces[i - side, at, :].astype(F32)
            j = i + GAUGE - side
            if j < chans:
                high = traces[j, at, :].astype(F32)
                if i < side:
                    high = jnp.where(me == 0, 0.0, high)
            else:
                high = jnp.where(me == n - 1, 0.0, nxt[j - chans, at, :].astype(F32))
            diff = high - low
            scale = lax.rsqrt(jnp.sum(diff * diff, axis=1, keepdims=True) * (1.0 / length) + 1e-05)
            norm_buf[pl.ds(i * gw, gw), :] = (diff * scale).astype(BF16)
        normed = norm_buf[...]
        re = lax.dot_general(table[pl.ds(0, F), :], normed, NT, preferred_element_type=F32)
        im = lax.dot_general(table[pl.ds(F, F), :], normed, NT, preferred_element_type=F32)
        magnitude = jnp.sqrt(re * re + im * im).astype(BF16)
        smooth = jnp.dot(band[...], magnitude, preferred_element_type=F32) * per_count
        gain = 1.0 / (smooth + 1e-06)
        white = (re * gain, im * gain)
        for tile in range(2):
            q = [white[p % 2][(p // 2) * n:(p // 2 + 1) * n, tile * 128:(tile + 1) * 128] for p in range(8)]
            for bit in range(3):
                step = gw << bit
                upper = (lane // step) % 2 == 1
                fresh = list(q)
                for p in range(8):
                    if p & (1 << bit):
                        continue
                    a, b = q[p], q[p | (1 << bit)]
                    fresh[p] = jnp.where(upper, pltpu.roll(b, step, 1), a)
                    fresh[p | (1 << bit)] = jnp.where(upper, b, pltpu.roll(a, 128 - step, 1))
                q = fresh
            for c in range(8):
                mixed[pl.ds(tile * 8 + c, n, stride=chans), :] = q[c]
        sent[g] = mixed[...].astype(BF16).reshape(n, chans, 128)

        def send(d, c):
            peer = lax.rem(me + d, n)
            pltpu.make_async_remote_copy(
                src_ref=sent.at[g, peer], dst_ref=held.at[g, me], send_sem=a2a_send.at[g], recv_sem=a2a_recv.at[g],
                device_id={"chan": peer}, device_id_type=MESH).start()
            return c

        lax.fori_loop(1, n, send, 0)
        held[g, me] = sent[g, me]
        return carry

    lax.fori_loop(0, groups, whiten, 0)

    per_tile = 16
    row_tiles = []
    sub = lax.broadcasted_iota(jnp.int32, (8, 1), 0)
    owners = (win, y_peer, core_peer, lax.rem(core_peer + 2, 4))
    column = lax.broadcasted_iota(jnp.int32, (8, n * chans), 1)
    for t in range(4):
        for half in range(per_tile // 8):
            ids = jnp.zeros((8, 1), jnp.int32)
            for r in range(8):
                ids = jnp.where(sub == r, index_ref[owners[t] * per_tile + half * 8 + r], ids)
            ids = lax.rem(ids + side, n * chans)
            row_tiles.append((column == ids).astype(F32))
    picker = jnp.concatenate(row_tiles, axis=0).astype(BF16)
    lane16 = lax.broadcasted_iota(jnp.int32, (per_tile, 128), 1)
    is_im = (lane16 // gw) % 2 == 1

    def all_received(g):
        return pltpu.make_async_remote_copy(
            src_ref=sent.at[g, pl.ds(0, n - 1)], dst_ref=held.at[g, pl.ds(0, n - 1)], send_sem=a2a_send.at[g],
            recv_sem=a2a_recv.at[g], device_id={"chan": right}, device_id_type=MESH)

    rows = n * chans
    part = rows // parts

    for g in range(groups):
        all_received(g).wait_recv()
        block = held[g].reshape(rows, 128)
        picked = jnp.dot(picker, block, preferred_element_type=F32)
        pieces = []
        for t in range(4):
            pk = picked[t * per_tile:(t + 1) * per_tile]
            swapped = jnp.where(is_im, -pltpu.roll(pk, gw, 1), pltpu.roll(pk, 128 - gw, 1))
            for q in range(4):
                own = (lane16 // (2 * gw)) == q
                pieces.append(jnp.where(own, pk, 0.0))
                pieces.append(jnp.where(own, swapped, 0.0))
        weights = jnp.concatenate(pieces, axis=0).astype(BF16)
        for r in range(parts):
            at = pl.ds(r * part, part)
            rows_in = held[g, pl.ds(r * (n // parts), n // parts)].reshape(part, 128)
            term = lax.dot_general(rows_in, weights, NT, preferred_element_type=F32)
            acc[at, :] = term if g == 0 else acc[at, :] + term
    acc[pl.ds(rows, 8), :] = acc[pl.ds(0, 8), :]

    def core_copy(r):
        at = pl.ds(r * part, part)
        return pltpu.make_async_remote_copy(
            src_ref=core_out.at[:, at], dst_ref=core_in.at[:, at], send_sem=core_send.at[r], recv_sem=core_recv.at[r],
            device_id={"win": core_peer}, device_id_type=MESH)

    def y_copy(r):
        at = pl.ds(r * part, part)
        return pltpu.make_async_remote_copy(
            src_ref=y_out.at[at], dst_ref=y_in.at[at], send_sem=y_send.at[r], recv_sem=y_recv.at[r],
            device_id={"win": y_peer}, device_id_type=MESH)

    for r in range(parts):
        at, shifted = pl.ds(r * part, part), pl.ds(r * part + side, part)
        core_out[0, at, :] = acc[shifted, 256:384].astype(BF16)
        core_out[1, at, :] = acc[shifted, 384:512].astype(BF16)
        core_copy(r).start()
    for r in range(parts):
        at, shifted = pl.ds(r * part, part), pl.ds(r * part + side, part)
        core_copy(r).wait_recv()
        y_out[at, :] = (acc[shifted, 128:256] + core_in[1, at, :].astype(F32)).astype(BF16)
        y_copy(r).start()
    per_part = n // parts
    for r in range(parts):
        at, shifted = pl.ds(r * part, part), pl.ds(r * part + side, part)
        y_copy(r).wait_recv()
        total = acc[shifted, 0:128] + core_in[0, at, :].astype(F32) + y_in[at, :].astype(F32)
        back_out[pl.ds(r * per_part, per_part)] = (total * (1.0 / (wins * 4))).astype(BF16).reshape(per_part, chans, 128)

        def give(d, c):
            peer = r * per_part + lax.rem(me + d, per_part)

            @pl.when(peer != me)
            def _():
                pltpu.make_async_remote_copy(
                    src_ref=back_out.at[peer], dst_ref=back_in.at[me], send_sem=back_send, recv_sem=back_recv,
                    device_id={"chan": peer}, device_id_type=MESH).start()

            return c

        lax.fori_loop(0, per_part, give, 0)
    back_in[me] = back_out[me]
    back = pltpu.make_async_remote_copy(
        src_ref=back_out.at[pl.ds(0, n - 1)], dst_ref=back_in.at[pl.ds(0, n - 1)], send_sem=back_send, recv_sem=back_recv,
        device_id={"chan": right}, device_id_type=MESH)
    back.wait_recv()
    back_f32[...] = back_in[...].reshape(rows, 128).astype(F32)
    for c in range(chans):
        flipped = back_f32[pl.ds(c, n, stride=chans), :].T
        for half in range(2):
            both = jnp.concatenate([flipped[half * 64:half * 64 + 32], flipped[half * 64 + 32:half * 64 + 64]], axis=1)
            halves[half, pl.ds(c, 32, stride=chans), :] = both
    out_ref[:, pl.ds(0, 128)] = halves[0]
    out_ref[:, pl.ds(128, 128)] = halves[1]
    for g in range(groups):
        all_received(g).wait_send()
    for r in range(parts):
        core_copy(r).wait_send()
        y_copy(r).wait_send()
    back.wait_send()


def solution(mesh):
    n = mesh.shape["chan"]

    def per_device(traces, source_index):
        chans, wins, length = traces.shape
        groups, parts = 3, 4
        gw = wins // groups
        rows = n * chans
        vmem = pl.BlockSpec(memory_space=pltpu.VMEM)
        out = pl.pallas_call(
            functools.partial(body, n, (chans, wins, length, groups, parts)),
            out_shape=jax.ShapeDtypeStruct((2 * 16 * chans, F), F32),
            in_specs=[pl.BlockSpec(memory_space=pltpu.SMEM), vmem, vmem, vmem],
            out_specs=vmem,
            scratch_shapes=[
                pltpu.VMEM((GAUGE // 2, wins, length), BF16),
                pltpu.VMEM((GAUGE // 2, wins, length), BF16),
                pltpu.VMEM((chans * gw, length), BF16),
                pltpu.VMEM((rows, 128), F32),
                pltpu.VMEM((groups, n, chans, 128), BF16),
                pltpu.VMEM((groups, n, chans, 128), BF16),
                pltpu.VMEM((rows + 8, 512), F32),
                pltpu.VMEM((2, rows, 128), BF16),
                pltpu.VMEM((2, rows, 128), BF16),
                pltpu.VMEM((rows, 128), BF16),
                pltpu.VMEM((rows, 128), BF16),
                pltpu.VMEM((n, chans, 128), BF16),
                pltpu.VMEM((n, chans, 128), BF16),
                pltpu.VMEM((rows, 128), F32),
                pltpu.VMEM((2, 2 * 16 * chans, 128), F32),
                pltpu.SemaphoreType.DMA((groups, 2)),
                pltpu.SemaphoreType.DMA((groups, 2)),
                pltpu.SemaphoreType.DMA((groups,)),
                pltpu.SemaphoreType.DMA((groups,)),
                pltpu.SemaphoreType.DMA((parts,)),
                pltpu.SemaphoreType.DMA((parts,)),
                pltpu.SemaphoreType.DMA((parts,)),
                pltpu.SemaphoreType.DMA((parts,)),
                pltpu.SemaphoreType.DMA,
                pltpu.SemaphoreType.DMA,
            ],
            compiler_params=pltpu.CompilerParams(
                collective_id=0, has_side_effects=True, vmem_limit_bytes=48 * 2**20
            ),
        )(source_index, traces, jnp.asarray(make_table(length)), jnp.asarray(make_band()))
        return out.reshape(2, 16, chans, F)

    return jax.shard_map(
        per_device,
        mesh=mesh,
        in_specs=(P("chan", "win", None), P()),
        out_specs=P(None, "win", "chan", None),
        check_vma=False,
    )
```

time: 496 us -> 63.4 us (0.13)
  the two profiles are of different devices: /device:TPU:1 before, /device:TPU:6 now
where the time goes in v1:
time: 63.4 us; the launch traced here: 63.2 us
  Pallas kernels  57.8 us (91%)
  local copies, waits for them, and re-layouts  5.43 us (9%)
    pallas_call x1, Pallas kernels, per_device(): pl.pallas_call(functools.partial(body, n, (chans, wins, length, groups, p...  57.8 us
    unnamed x9, local copies, waits for them, and re-layouts  5.43 us

profile of v1, /device:TPU:6, one launch (start us, length us, event | category | flops | bytes accessed | tf_op | source)
XLA Modules:
  0.0 63.2 jit_solution(12792585527364317247)
XLA Ops:
  0.0 0.0 copy-start
  0.0 1.7 %copy-done = bf16[16,48,1500]{2,1,0:T(8,128)(2,1)S(1)} copy-done((bf16[16,48,1500]{2,1,0:T(8,128)(2,1)S(1)}, bf16[16,48,1500]{2,1,0:T(8,128)(2,1)}, u32[]{:S(2)}) %copy-start) | copy-done | bytes 2304024
  1.7 0.0 copy-start.1
  1.7 1.4 %copy-done.1 = bf16[512,1500]{1,0:T(8,128)(2,1)S(1)} copy-done((bf16[512,1500]{1,0:T(8,128)(2,1)S(1)}, bf16[512,1500]{1,0:T(8,128)(2,1)}, u32[]{:S(2)}) %copy-start.1) | copy-done | bytes 1536024
  3.1 0.0 copy-start.2
  3.1 0.9 %copy-done.2 = bf16[256,256]{1,0:T(8,128)(2,1)S(1)} copy-done((bf16[256,256]{1,0:T(8,128)(2,1)S(1)}, bf16[256,256]{1,0:T(8,128)(2,1)}, u32[]{:S(2)}) %copy-start.2) | copy-done | bytes 131096
  4.0 0.0 copy-start.3
  4.0 0.7 %copy-done.3 = s32[64]{0:T(128)S(1)} copy-done((s32[64]{0:T(128)S(1)}, s32[64]{0:T(128)}, u32[]{:S(2)}) %copy-start.3) | copy-done | bytes 280
  4.6 57.8 %shard_map.46 = f32[512,256]{1,0:T(8,128)S(1)} custom-call(s32[64]{0:T(128)S(1)} %copy-done.3, bf16[16,48,1500]{2,1,0:T(8,128)(2,1)S(1)} %copy-done, bf16[512,1500]{1,0:T(8,128)(2,1)S(1)} %copy-done.1, bf16[256,256]{1,0:T(8,128)(2,1)S(1)} %copy-done.2), custom_call_target="tpu_custom_call" | custom-call | tf_op jit(solution)/shard_map/pallas_call | solution.py:250
  62.4 0.8 %copy.6 = f32[2,16,16,256]{3,2,1,0:T(8,128)} copy(f32[2,16,16,256]{3,2,1,0:T(8,128)S(1)} %bitcast.1) | data formatting | bytes 1048576
Async XLA Ops:
  0.0 1.7 %copy-start = (bf16[16,48,1500]{2,1,0:T(8,128)(2,1)S(1)}, bf16[16,48,1500]{2,1,0:T(8,128)(2,1)}, u32[]{:S(2)}) copy-start(bf16[16,48,1500]{2,1,0:T(8,128)(2,1)} %traces.1) | copy-start | bytes 6912004
  1.7 1.4 %copy-start.1 = (bf16[512,1500]{1,0:T(8,128)(2,1)S(1)}, bf16[512,1500]{1,0:T(8,128)(2,1)}, u32[]{:S(2)}) copy-start(bf16[512,1500]{1,0:T(8,128)(2,1)} %constant.4.clone.table) | copy-start | bytes 4608004
  3.1 0.9 %copy-start.2 = (bf16[256,256]{1,0:T(8,128)(2,1)S(1)}, bf16[256,256]{1,0:T(8,128)(2,1)}, u32[]{:S(2)}) copy-start(bf16[256,256]{1,0:T(8,128)(2,1)} %constant.5.clone.band) | copy-start | bytes 393220
  4.0 0.7 %copy-start.3 = (s32[64]{0:T(128)S(1)}, s32[64]{0:T(128)}, u32[]{:S(2)}) copy-start(s32[64]{0:T(128)} %index_ref.1) | copy-start | bytes 772

commit v2 on v1

v2 whole, which is shorter than its diff:
```python
import functools
import math

import jax
import jax.numpy as jnp
import ml_dtypes
import numpy as np
from jax import lax
from jax.experimental import pallas as pl
from jax.experimental.pallas import tpu as pltpu
from jax.sharding import PartitionSpec as P

F = 256
F0 = 1
K = 64
GAUGE = 4
MESH = pl.DeviceIdType.MESH
BF16 = jnp.bfloat16
F32 = jnp.float32
NT = (((1,), (1,)), ((), ()))


def make_table(length):
    times = np.arange(length, dtype=np.int64)[None, :]
    bins = np.arange(F, dtype=np.int64)[:, None] + F0
    phase = (times * bins % length).astype(np.float32) * np.float32(2.0 * math.pi / length)
    phase = phase.astype(np.float64)
    band = np.zeros((F, length))
    band[:, :F] = np.abs(np.arange(F)[:, None] - np.arange(F)[None, :]) <= K
    return np.concatenate([np.cos(phase), -np.sin(phase), band], axis=0).astype(np.float32).astype(ml_dtypes.bfloat16)


def make_picker(index_ref, picker, owners, rows):
    sub = lax.broadcasted_iota(jnp.int32, (8, 1), 0)
    column = lax.broadcasted_iota(jnp.int32, (8, rows), 1)
    for t, owner in enumerate(owners):
        tiles = []
        for half in range(2):
            ids = jnp.zeros((8, 1), jnp.int32)
            for r in range(8):
                ids = jnp.where(sub == r, index_ref[owner * 16 + half * 8 + r], ids)
            tiles.append((column == ids).astype(F32))
        picker[pl.ds(t * 16, 16), :] = jnp.concatenate(tiles, axis=0).astype(BF16)


def body(n, sizes, index_ref, traces_hbm, table_hbm, near_ref, far_ref, traces, table, band, picker, load_sem, prev, nxt, norm_buf,
         mixed, sent, held, other, acc, y_out, y_in, back_out, back_in, far_out, far_in, halo_send, halo_recv, a2a_send,
         a2a_recv, core_send, core_recv, y_send, y_recv, back_send, back_recv, far_send,
         far_recv, group_sem, all_sem):
    chans, wins, length, groups, parts = sizes
    side = GAUGE // 2
    gw = wins // groups
    rows = n * chans
    me = lax.axis_index("chan")
    win = lax.axis_index("win")
    core_peer = win + 1 - 2 * lax.rem(win, 2)
    y_peer = lax.rem(win + 2, 4)
    right, left = lax.rem(me + 1, n), lax.rem(me + n - 1, n)

    barrier = pltpu.get_barrier_semaphore()

    line = 8
    far_in[...] = jnp.zeros_like(far_in)
    for d in range(1, line):
        pl.semaphore_signal(
            barrier, inc=1, device_id={"chan": me // line * line + lax.rem(me + d, line)}, device_id_type=MESH)
        pl.semaphore_signal(barrier, inc=1, device_id={"chan": lax.rem(me + line * d, n)}, device_id_type=MESH)
    for peer in (left, right):
        pl.semaphore_signal(barrier, inc=1, device_id={"chan": peer}, device_id_type=MESH)
    for peer in (core_peer, y_peer):
        pl.semaphore_signal(barrier, inc=1, device_id={"win": peer}, device_id_type=MESH)

    def load(g):
        at = pl.ds(g * gw, gw)
        return pltpu.make_async_copy(traces_hbm.at[:, at], traces.at[:, at], load_sem.at[g])

    load_table = pltpu.make_async_copy(table_hbm.at[pl.ds(0, 2 * F)], table, load_sem.at[groups])
    load_band = pltpu.make_async_copy(table_hbm.at[pl.ds(2 * F, F), pl.ds(0, F)], band, load_sem.at[groups + 1])
    load(0).start()
    load_table.start()
    load_band.start()
    for g in range(1, groups):
        load(g).start()
    make_picker(index_ref, picker, (win, y_peer), rows)
    pl.semaphore_wait(barrier, 2 * line + 2)

    def halo(g, way):
        at = pl.ds(pl.multiple_of(g * gw, gw), gw)
        if way == 0:
            return pltpu.make_async_remote_copy(
                src_ref=traces_hbm.at[pl.ds(0, side), at], dst_ref=nxt.at[:, at], send_sem=halo_send.at[g, 0],
                recv_sem=halo_recv.at[g, 0], device_id={"chan": left}, device_id_type=MESH)
        return pltpu.make_async_remote_copy(
            src_ref=traces_hbm.at[pl.ds(chans - side, side), at], dst_ref=prev.at[:, at], send_sem=halo_send.at[g, 1],
            recv_sem=halo_recv.at[g, 1], device_id={"chan": right}, device_id_type=MESH)

    for g in range(groups):
        for way in range(2):
            halo(g, way).start()
    for d in range(1, line):
        pl.semaphore_signal(
            group_sem, inc=1, device_id={"chan": me // line * line + lax.rem(me + d, line)}, device_id_type=MESH)
    load_table.wait()
    load_band.wait()
    for g in range(groups):
        load(g).wait()

    bins = lax.broadcasted_iota(jnp.int32, (F, 1), 0)
    counts = jnp.minimum(bins + K, F - 1) - jnp.maximum(bins - K, 0) + 1
    per_count = 1.0 / counts.astype(F32)
    lane = lax.broadcasted_iota(jnp.int32, (n, 128), 1)

    def normalise(g, i):
        at = pl.ds(pl.multiple_of(g * gw, gw), gw)
        if i < chans - side:
            low = traces[i, at, :].astype(F32)
            if i + GAUGE < chans:
                high = traces[i + GAUGE, at, :].astype(F32)
            else:
                high = jnp.where(me == n - 1, 0.0, nxt[i + GAUGE - chans, at, :].astype(F32))
        else:
            low = prev[i - chans + side, at, :].astype(F32)
            high = jnp.where(me == 0, 0.0, traces[i - chans + GAUGE, at, :].astype(F32))
        diff = high - low
        scale = lax.rsqrt(jnp.sum(diff * diff, axis=1, keepdims=True) * (1.0 / length) + 1e-05)
        norm_buf[g, pl.ds(i * gw, gw), :] = (diff * scale).astype(BF16)

    def whiten(g, tile):
        normed = norm_buf[g, pl.ds(tile * 128, 128), :]
        re = lax.dot_general(table[pl.ds(0, F), :], normed, NT, preferred_element_type=F32)
        im = lax.dot_general(table[pl.ds(F, F), :], normed, NT, preferred_element_type=F32)
        magnitude = jnp.sqrt(re * re + im * im).astype(BF16)
        smooth = jnp.dot(band[...], magnitude, preferred_element_type=F32) * per_count
        gain = 1.0 / (smooth + 1e-06)
        white = (re * gain, im * gain)
        q = [white[p % 2][(p // 2) * n:(p // 2 + 1) * n] for p in range(8)]
        for bit in range(3):
            step = gw << bit
            upper = (lane // step) % 2 == 1
            fresh = list(q)
            for p in range(8):
                if p & (1 << bit):
                    continue
                a, b = q[p], q[p | (1 << bit)]
                fresh[p] = jnp.where(upper, pltpu.roll(b, step, 1), a)
                fresh[p | (1 << bit)] = jnp.where(upper, b, pltpu.roll(a, 128 - step, 1))
            q = fresh
        for c in range(8):
            mixed[g, pl.ds(tile * 8 + c, n, stride=chans), :] = q[c]

    def before(g, carry):
        for i in range(chans - GAUGE):
            normalise(g, i)
        whiten(g, 0)
        return carry

    lax.fori_loop(0, groups, before, 0)
    pl.semaphore_wait(group_sem, line - 1)
    pl.semaphore_signal(all_sem, inc=1, device_id={"win": y_peer}, device_id_type=MESH)

    def after(g, carry):
        halo(g, 0).wait()
        halo(g, 1).wait()
        for i in range(chans - GAUGE, chans):
            normalise(g, i)
        whiten(g, 1)
        sent[g] = mixed[g].astype(BF16).reshape(n, chans, 128)

        def send(d, c):
            peer = lax.rem(me + d, n)
            pltpu.make_async_remote_copy(
                src_ref=sent.at[g, peer], dst_ref=held.at[g, me], send_sem=a2a_send.at[g], recv_sem=a2a_recv.at[g],
                device_id={"chan": peer}, device_id_type=MESH).start()
            return c

        lax.fori_loop(1, n, send, 0)
        held[g, me] = sent[g, me]
        return carry

    lax.fori_loop(0, groups, after, 0)

    def all_received(g):
        return pltpu.make_async_remote_copy(
            src_ref=sent.at[g, pl.ds(0, n - 1)], dst_ref=held.at[g, pl.ds(0, n - 1)], send_sem=a2a_send.at[g],
            recv_sem=a2a_recv.at[g], device_id={"chan": right}, device_id_type=MESH)

    def forward(g):
        return pltpu.make_async_remote_copy(
            src_ref=held.at[g], dst_ref=other.at[g], send_sem=core_send.at[g], recv_sem=core_recv.at[g],
            device_id={"win": core_peer}, device_id_type=MESH)

    lane16 = lax.broadcasted_iota(jnp.int32, (16, 128), 1)
    is_im = (lane16 // gw) % 2 == 1
    own_row = lax.broadcasted_iota(jnp.int32, (n, chans, 128), 1) < chans - side

    def straight(block):
        block = block.astype(F32)
        following = jnp.concatenate([block[1:], block[:1]], axis=0)
        return jnp.where(own_row, block, following).reshape(rows, 128).astype(BF16)

    def weights_of(block):
        picked = jnp.dot(picker[...], block, preferred_element_type=F32)
        pieces = []
        for t in range(2):
            pk = picked[t * 16:(t + 1) * 16]
            swapped = jnp.where(is_im, -pltpu.roll(pk, gw, 1), pltpu.roll(pk, 128 - gw, 1))
            for q in range(4):
                mine = (lane16 // (2 * gw)) == q
                pieces.append(jnp.where(mine, pk, 0.0))
                pieces.append(jnp.where(mine, swapped, 0.0))
        return jnp.concatenate(pieces, axis=0).astype(BF16)

    blocks, weights = [], []
    for g in range(groups):
        all_received(g).wait_recv()
        forward(g).start()
        for source in (held, other):
            if source is other:
                forward(g).wait_recv()
            blocks.append(straight(source[g]))
            weights.append(weights_of(blocks[-1]))
        block = jnp.concatenate(blocks[-2:], axis=1)
        weight = jnp.concatenate(weights[-2:], axis=1)
        term = lax.dot_general(block, weight, NT, preferred_element_type=F32)
        if g == 0:
            acc[...] = term
        else:
            acc[...] += term

    part = rows // parts
    per_part = n // parts
    first_peer = me // (n // 4) * (n // 4)

    def base(r):
        return lax.rem(first_peer + r * per_part, n)

    def at(r):
        return pl.ds(pl.multiple_of(base(r) * chans, part), part)

    def y_copy(r):
        return pltpu.make_async_remote_copy(
            src_ref=y_out.at[at(r)], dst_ref=y_in.at[at(r)], send_sem=y_send.at[r], recv_sem=y_recv.at[r],
            device_id={"win": y_peer}, device_id_type=MESH)

    summed = [r for r in range(parts) if r // (parts // 4) % 2 == 0]
    direct = [r for r in range(parts) if r not in summed]
    share = 1.0 / (wins * 4)

    def give(r, source, target, to_win, sems, skip):
        def one(d, c):
            peer = base(r) + lax.rem(me + d, per_part)

            def start():
                pltpu.make_async_remote_copy(
                    src_ref=source.at[peer], dst_ref=target.at[me], send_sem=sems[0], recv_sem=sems[1],
                    device_id={"chan": peer, "win": to_win}, device_id_type=MESH).start()

            if skip:
                pl.when(peer != me)(start)
            else:
                start()
            return c

        lax.fori_loop(0, per_part, one, 0)

    def tiles(value):
        return (value * share).astype(BF16).reshape(per_part, chans, 128)

    for r in summed:
        y_out[at(r), :] = acc[at(r), 128:256].astype(BF16)
        y_copy(r).start()
    pl.semaphore_wait(all_sem, 1)
    for r in direct:
        back_out[pl.ds(base(r), per_part)] = tiles(acc[at(r), 0:128])
        give(r, back_out, back_in, win, (back_send, back_recv), False)
        far_out[pl.ds(base(r), per_part)] = tiles(acc[at(r), 128:256])
        give(r, far_out, far_in, y_peer, (far_send, far_recv), False)
    for r in summed:
        y_copy(r).wait_recv()
        back_out[pl.ds(base(r), per_part)] = tiles(acc[at(r), 0:128] + y_in[at(r), :].astype(F32))
        give(r, back_out, back_in, win, (back_send, back_recv), r // (parts // 4) == 0)
    back_in[me] = back_out[me]

    def all_back(source, target, count, sems):
        return pltpu.make_async_remote_copy(
            src_ref=source.at[pl.ds(0, count)], dst_ref=target.at[pl.ds(0, count)], send_sem=sems[0], recv_sem=sems[1],
            device_id={"chan": right}, device_id_type=MESH)

    back = all_back(back_out, back_in, n - 1, (back_send, back_recv))
    far = all_back(far_out, far_in, n // 2, (far_send, far_recv))
    back.wait_recv()
    far.wait_recv()
    near_ref[...] = back_in[...]
    far_ref[...] = far_in[...]
    for g in range(groups):
        all_received(g).wait_send()
        forward(g).wait_send()
    for r in summed:
        y_copy(r).wait_send()
    back.wait_send()
    far.wait_send()


def arrange(near, far, out_ref, back_f32, halves):
    n, chans, _ = near.shape
    back_f32[...] = (near[...].astype(F32) + far[...].astype(F32)).reshape(n * chans, 128)
    for c in range(chans):
        flipped = back_f32[pl.ds(c, n, stride=chans), :].T
        for half in range(2):
            both = jnp.concatenate([flipped[half * 64:half * 64 + 32], flipped[half * 64 + 32:half * 64 + 64]], axis=1)
            halves[half, pl.ds(c, 32, stride=chans), :] = both
    out_ref[:, pl.ds(0, 128)] = halves[0]
    out_ref[:, pl.ds(128, 128)] = halves[1]


def solution(mesh):
    n = mesh.shape["chan"]

    def per_device(traces, source_index):
        chans, wins, length = traces.shape
        groups, parts = 3, 8
        gw = wins // groups
        rows = n * chans
        vmem = pl.BlockSpec(memory_space=pltpu.VMEM)
        hbm = pl.BlockSpec(memory_space=pltpu.HBM)
        near, far = pl.pallas_call(
            functools.partial(body, n, (chans, wins, length, groups, parts)),
            out_shape=[jax.ShapeDtypeStruct((n, chans, 128), BF16)] * 2,
            in_specs=[pl.BlockSpec(memory_space=pltpu.SMEM), hbm, hbm],
            out_specs=[vmem, vmem],
            scratch_shapes=[
                pltpu.VMEM((chans, wins, length), BF16),
                pltpu.VMEM((2 * F, length), BF16),
                pltpu.VMEM((F, F), BF16),
                pltpu.VMEM((2 * 16, rows), BF16),
                pltpu.SemaphoreType.DMA((groups + 2,)),
                pltpu.VMEM((GAUGE // 2, wins, length), BF16),
                pltpu.VMEM((GAUGE // 2, wins, length), BF16),
                pltpu.VMEM((groups, chans * gw, length), BF16),
                pltpu.VMEM((groups, rows, 128), F32),
                pltpu.VMEM((groups, n, chans, 128), BF16),
                pltpu.VMEM((groups, n, chans, 128), BF16),
                pltpu.VMEM((groups, n, chans, 128), BF16),
                pltpu.VMEM((rows, 256), F32),
                pltpu.VMEM((rows, 128), BF16),
                pltpu.VMEM((rows, 128), BF16),
                pltpu.VMEM((n, chans, 128), BF16),
                pltpu.VMEM((n, chans, 128), BF16),
                pltpu.VMEM((n, chans, 128), BF16),
                pltpu.VMEM((n, chans, 128), BF16),
                pltpu.SemaphoreType.DMA((groups, 2)),
                pltpu.SemaphoreType.DMA((groups, 2)),
                pltpu.SemaphoreType.DMA((groups,)),
                pltpu.SemaphoreType.DMA((groups,)),
                pltpu.SemaphoreType.DMA((groups,)),
                pltpu.SemaphoreType.DMA((groups,)),
                pltpu.SemaphoreType.DMA((parts,)),
                pltpu.SemaphoreType.DMA((parts,)),
                pltpu.SemaphoreType.DMA,
                pltpu.SemaphoreType.DMA,
                pltpu.SemaphoreType.DMA,
                pltpu.SemaphoreType.DMA,
                pltpu.SemaphoreType.REGULAR,
                pltpu.SemaphoreType.REGULAR,
            ],
            compiler_params=pltpu.CompilerParams(
                collective_id=0, has_side_effects=True, vmem_limit_bytes=62 * 2**20
            ),
        )(source_index, traces, jnp.asarray(make_table(length)))
        out = pl.pallas_call(
            arrange,
            out_shape=jax.ShapeDtypeStruct((2 * 16 * chans, F), F32),
            in_specs=[vmem, vmem],
            out_specs=vmem,
            scratch_shapes=[pltpu.VMEM((rows, 128), F32), pltpu.VMEM((2, 2 * 16 * chans, 128), F32)],
        )(near, far)
        return out.reshape(2, 16, chans, F)

    return jax.shard_map(
        per_device,
        mesh=mesh,
        in_specs=(P("chan", "win", None), P()),
        out_specs=P(None, "win", "chan", None),
        check_vma=False,
    )
```

time: 63.4 us -> 57.4 us (0.905)
  the two profiles are of different devices: /device:TPU:6 before, /device:TPU:1 now
where the time goes in v2:
time: 57.4 us; the launch traced here: 57.3 us
  Pallas kernels  57.3 us (100%)
    pallas_call x1, Pallas kernels, per_device(): pl.pallas_call(functools.partial(body, n, (chans, wins, length, groups, p...  54.8 us
    pallas_call x1, Pallas kernels, per_device(): pl.pallas_call(arrange, out_shape=jax.ShapeDtypeStruct((2 * 16 * chans, F...  2.49 us

profile of v2, /device:TPU:1, one launch (start us, length us, event | category | flops | bytes accessed | tf_op | source)
XLA Modules:
  0.0 57.3 jit_solution(14268319803575937236)
XLA Ops:
  0.0 54.8 %shard_map.37 = (bf16[64,16,128]{2,1,0:T(8,128)(2,1)}, bf16[64,16,128]{2,1,0:T(8,128)(2,1)}) custom-call(s32[64]{0:T(128)} %index_ref.1, bf16[16,48,1500]{2,1,0:T(8,128)(2,1)} %traces_hbm.1, bf16[768,1500]{1,0:T(8,128)(2,1)} %constant.2.clone.table_hbm), custom_call_target="tpu_custom_call" | custom-call | tf_op jit(solution)/shard_map/pallas_call | solution.py:326
  54.8 2.5 %shard_map.38 = f32[512,256]{1,0:T(8,128)} custom-call(bf16[64,16,128]{2,1,0:T(8,128)(2,1)} %get-tuple-element.7.near, bf16[64,16,128]{2,1,0:T(8,128)(2,1)} %get-tuple-element.8.far), custom_call_target="tpu_custom_call" | custom-call | tf_op jit(solution)/shard_map/pallas_call | solution.py:370

commit v3 on v2

--- a/solution.py
+++ b/solution.py
@@ -43,10 +43,10 @@
         picker[pl.ds(t * 16, 16), :] = jnp.concatenate(tiles, axis=0).astype(BF16)
 
 
-def body(n, sizes, index_ref, traces_hbm, table_hbm, near_ref, far_ref, traces, table, band, picker, load_sem, prev, nxt, norm_buf,
+def body(n, sizes, index_ref, traces_hbm, table_hbm, out_ref, traces, table, band, picker, load_sem, prev, nxt, norm_buf,
          mixed, sent, held, other, acc, y_out, y_in, back_out, back_in, far_out, far_in, halo_send, halo_recv, a2a_send,
          a2a_recv, core_send, core_recv, y_send, y_recv, back_send, back_recv, far_send,
-         far_recv, group_sem, all_sem):
+         far_recv, group_sem, all_sem, back_f32, halves):
     chans, wins, length, groups, parts = sizes
     side = GAUGE // 2
     gw = wins // groups
@@ -242,7 +242,7 @@
             src_ref=y_out.at[at(r)], dst_ref=y_in.at[at(r)], send_sem=y_send.at[r], recv_sem=y_recv.at[r],
             device_id={"win": y_peer}, device_id_type=MESH)
 
-    summed = [r for r in range(parts) if r // (parts // 4) % 2 == 0]
+    summed = [r for r in range(parts) if r // (parts // 4) % 2 == 1]
     direct = [r for r in range(parts) if r not in summed]
     share = 1.0 / (wins * 4)
 
@@ -272,13 +272,13 @@
     pl.semaphore_wait(all_sem, 1)
     for r in direct:
         back_out[pl.ds(base(r), per_part)] = tiles(acc[at(r), 0:128])
-        give(r, back_out, back_in, win, (back_send, back_recv), False)
+        give(r, back_out, back_in, win, (back_send, back_recv), r // (parts // 4) == 0)
         far_out[pl.ds(base(r), per_part)] = tiles(acc[at(r), 128:256])
         give(r, far_out, far_in, y_peer, (far_send, far_recv), False)
     for r in summed:
         y_copy(r).wait_recv()
         back_out[pl.ds(base(r), per_part)] = tiles(acc[at(r), 0:128] + y_in[at(r), :].astype(F32))
-        give(r, back_out, back_in, win, (back_send, back_recv), r // (parts // 4) == 0)
+        give(r, back_out, back_in, win, (back_send, back_recv), False)
     back_in[me] = back_out[me]
 
     def all_back(source, target, count, sems):
@@ -290,8 +290,7 @@
     far = all_back(far_out, far_in, n // 2, (far_send, far_recv))
     back.wait_recv()
     far.wait_recv()
-    near_ref[...] = back_in[...]
-    far_ref[...] = far_in[...]
+    arrange(back_in, far_in, out_ref, back_f32, halves)
     for g in range(groups):
         all_received(g).wait_send()
         forward(g).wait_send()
@@ -323,11 +322,11 @@
         rows = n * chans
         vmem = pl.BlockSpec(memory_space=pltpu.VMEM)
         hbm = pl.BlockSpec(memory_space=pltpu.HBM)
-        near, far = pl.pallas_call(
+        out = pl.pallas_call(
             functools.partial(body, n, (chans, wins, length, groups, parts)),
-            out_shape=[jax.ShapeDtypeStruct((n, chans, 128), BF16)] * 2,
+            out_shape=jax.ShapeDtypeStruct((2 * 16 * chans, F), F32),
             in_specs=[pl.BlockSpec(memory_space=pltpu.SMEM), hbm, hbm],
-            out_specs=[vmem, vmem],
+            out_specs=vmem,
             scratch_shapes=[
                 pltpu.VMEM((chans, wins, length), BF16),
                 pltpu.VMEM((2 * F, length), BF16),
@@ -362,18 +361,13 @@
                 pltpu.SemaphoreType.DMA,
                 pltpu.SemaphoreType.REGULAR,
                 pltpu.SemaphoreType.REGULAR,
+                pltpu.VMEM((rows, 128), F32),
+                pltpu.VMEM((2, 2 * 16 * chans, 128), F32),
             ],
             compiler_params=pltpu.CompilerParams(
-                collective_id=0, has_side_effects=True, vmem_limit_bytes=62 * 2**20
+                collective_id=0, has_side_effects=True, vmem_limit_bytes=52 * 2**20
             ),
         )(source_index, traces, jnp.asarray(make_table(length)))
-        out = pl.pallas_call(
-            arrange,
-            out_shape=jax.ShapeDtypeStruct((2 * 16 * chans, F), F32),
-            in_specs=[vmem, vmem],
-            out_specs=vmem,
-            scratch_shapes=[pltpu.VMEM((rows, 128), F32), pltpu.VMEM((2, 2 * 16 * chans, 128), F32)],
-        )(near, far)
         return out.reshape(2, 16, chans, F)
 
     return jax.shard_map(

time: 57.4 us -> 55.2 us (0.962)
  Pallas kernels: 57.3 us -> 53.7 us
  local copies, waits for them, and re-layouts: 0 us -> 1.45 us
    pallas_call x1 -> x0, Pallas kernels: 2.49 us -> none  [per_device(): pl.pallas_call(arrange, out_shape=jax.ShapeDtypeStruct((2 * 16 * chans, F...]
    unnamed x0 -> x3, local copies, waits for them, and re-layouts: none -> 1.45 us
    pallas_call x1, Pallas kernels: 54.8 us -> 53.7 us  [per_device(): pl.pallas_call(functools.partial(body, n, (chans, wins, length, groups, p...]
where the time goes in v3:
time: 55.2 us
  Pallas kernels  53.7 us (97%)
  local copies, waits for them, and re-layouts  1.45 us (3%)
    pallas_call x1, Pallas kernels, per_device(): pl.pallas_call(functools.partial(body, n, (chans, wins, length, groups, p...  53.7 us
    unnamed x3, local copies, waits for them, and re-layouts  1.45 us

profile of v3, /device:TPU:1, one launch (start us, length us, event | category | flops | bytes accessed | tf_op | source)
XLA Modules:
  0.0 55.2 jit_solution(11378827347825015074)
XLA Ops:
  0.0 0.0 copy-start
  0.0 0.7 %copy-done = s32[64]{0:T(128)S(1)} copy-done((s32[64]{0:T(128)S(1)}, s32[64]{0:T(128)}, u32[]{:S(2)}) %copy-start) | copy-done | bytes 280
  0.7 53.7 %shard_map.37 = f32[512,256]{1,0:T(8,128)S(1)} custom-call(s32[64]{0:T(128)S(1)} %copy-done, bf16[16,48,1500]{2,1,0:T(8,128)(2,1)} %traces_hbm.1, bf16[768,1500]{1,0:T(8,128)(2,1)} %constant.2.clone.table_hbm), custom_call_target="tpu_custom_call" | custom-call | tf_op jit(solution)/shard_map/pallas_call | solution.py:325
  54.4 0.8 %copy.5 = f32[2,16,16,256]{3,2,1,0:T(8,128)} copy(f32[2,16,16,256]{3,2,1,0:T(8,128)S(1)} %bitcast.1) | data formatting | bytes 1048576
Async XLA Ops:
  0.0 0.7 %copy-start = (s32[64]{0:T(128)S(1)}, s32[64]{0:T(128)}, u32[]{:S(2)}) copy-start(s32[64]{0:T(128)} %index_ref.1) | copy-start | bytes 772

commit v4 on v3

--- a/solution.py
+++ b/solution.py
@@ -167,7 +167,7 @@
         sent[g] = mixed[g].astype(BF16).reshape(n, chans, 128)
 
         def send(d, c):
-            peer = lax.rem(me + d, n)
+            peer = lax.rem(me + 5 * d, n)
             pltpu.make_async_remote_copy(
                 src_ref=sent.at[g, peer], dst_ref=held.at[g, me], send_sem=a2a_send.at[g], recv_sem=a2a_recv.at[g],
                 device_id={"chan": peer}, device_id_type=MESH).start()
@@ -317,7 +317,7 @@
 
     def per_device(traces, source_index):
         chans, wins, length = traces.shape
-        groups, parts = 3, 8
+        groups, parts = 3, 16
         gw = wins // groups
         rows = n * chans
         vmem = pl.BlockSpec(memory_space=pltpu.VMEM)

time: 55.2 us -> 54.2 us (0.982)
  Pallas kernels: 53.7 us -> 52.6 us
    pallas_call x1, Pallas kernels: 53.7 us -> 52.6 us  [per_device(): pl.pallas_call(functools.partial(body, n, (chans, wins, length, groups, p...]
where the time goes in v4:
time: 54.2 us; the launch traced here: 54.1 us
  Pallas kernels  52.6 us (97%)
  local copies, waits for them, and re-layouts  1.45 us (3%)
    pallas_call x1, Pallas kernels, per_device(): pl.pallas_call(functools.partial(body, n, (chans, wins, length, groups, p...  52.6 us
    unnamed x3, local copies, waits for them, and re-layouts  1.45 us

profile of v4, /device:TPU:1, one launch (start us, length us, event | category | flops | bytes accessed | tf_op | source)
XLA Modules:
  0.0 54.1 jit_solution(9316297000168886430)
XLA Ops:
  0.0 0.0 copy-start
  0.0 0.7 %copy-done = s32[64]{0:T(128)S(1)} copy-done((s32[64]{0:T(128)S(1)}, s32[64]{0:T(128)}, u32[]{:S(2)}) %copy-start) | copy-done | bytes 280
  0.7 52.6 %shard_map.37 = f32[512,256]{1,0:T(8,128)S(1)} custom-call(s32[64]{0:T(128)S(1)} %copy-done, bf16[16,48,1500]{2,1,0:T(8,128)(2,1)} %traces_hbm.1, bf16[768,1500]{1,0:T(8,128)(2,1)} %constant.2.clone.table_hbm), custom_call_target="tpu_custom_call" | custom-call | tf_op jit(solution)/shard_map/pallas_call | solution.py:325
  53.3 0.8 %copy.5 = f32[2,16,16,256]{3,2,1,0:T(8,128)} copy(f32[2,16,16,256]{3,2,1,0:T(8,128)S(1)} %bitcast.1) | data formatting | bytes 1048576
Async XLA Ops:
  0.0 0.7 %copy-start = (s32[64]{0:T(128)S(1)}, s32[64]{0:T(128)}, u32[]{:S(2)}) copy-start(s32[64]{0:T(128)} %index_ref.1) | copy-start | bytes 772

commit v5 on v4

--- a/solution.py
+++ b/solution.py
@@ -30,7 +30,7 @@
     return np.concatenate([np.cos(phase), -np.sin(phase), band], axis=0).astype(np.float32).astype(ml_dtypes.bfloat16)
 
 
-def make_picker(index_ref, picker, owners, rows):
+def make_picker(index_ref, picker, owners, rows, chans, side):
     sub = lax.broadcasted_iota(jnp.int32, (8, 1), 0)
     column = lax.broadcasted_iota(jnp.int32, (8, rows), 1)
     for t, owner in enumerate(owners):
@@ -39,6 +39,7 @@
             ids = jnp.zeros((8, 1), jnp.int32)
             for r in range(8):
                 ids = jnp.where(sub == r, index_ref[owner * 16 + half * 8 + r], ids)
+            ids = jnp.where(lax.rem(ids, chans) < chans - side, ids, lax.rem(ids + chans, rows))
             tiles.append((column == ids).astype(F32))
         picker[pl.ds(t * 16, 16), :] = jnp.concatenate(tiles, axis=0).astype(BF16)
 
@@ -81,7 +82,7 @@
     load_band.start()
     for g in range(1, groups):
         load(g).start()
-    make_picker(index_ref, picker, (win, y_peer), rows)
+    make_picker(index_ref, picker, (win, y_peer), rows, chans, side)
     pl.semaphore_wait(barrier, 2 * line + 2)
 
     def halo(g, way):
@@ -173,7 +174,7 @@
                 device_id={"chan": peer}, device_id_type=MESH).start()
             return c
 
-        lax.fori_loop(1, n, send, 0)
+        lax.fori_loop(1, n, send, 0, unroll=9)
         held[g, me] = sent[g, me]
         return carry
 
@@ -194,9 +195,8 @@
     own_row = lax.broadcasted_iota(jnp.int32, (n, chans, 128), 1) < chans - side
 
     def straight(block):
-        block = block.astype(F32)
         following = jnp.concatenate([block[1:], block[:1]], axis=0)
-        return jnp.where(own_row, block, following).reshape(rows, 128).astype(BF16)
+        return jnp.where(own_row, block, following).reshape(rows, 128)
 
     def weights_of(block):
         picked = jnp.dot(picker[...], block, preferred_element_type=F32)
@@ -218,7 +218,7 @@
             if source is other:
                 forward(g).wait_recv()
             blocks.append(straight(source[g]))
-            weights.append(weights_of(blocks[-1]))
+            weights.append(weights_of(source[g].reshape(rows, 128)))
         block = jnp.concatenate(blocks[-2:], axis=1)
         weight = jnp.concatenate(weights[-2:], axis=1)
         term = lax.dot_general(block, weight, NT, preferred_element_type=F32)
@@ -261,7 +261,7 @@
                 start()
             return c
 
-        lax.fori_loop(0, per_part, one, 0)
+        lax.fori_loop(0, per_part, one, 0, unroll=True)
 
     def tiles(value):
         return (value * share).astype(BF16).reshape(per_part, chans, 128)

time: 54.2 us -> 54.2 us (level)
  no operation moved by 1% of the time
where the time goes in v5:
time: 54.2 us; the launch traced here: 54.1 us
  Pallas kernels  52.6 us (97%)
  local copies, waits for them, and re-layouts  1.45 us (3%)
    pallas_call x1, Pallas kernels, per_device(): pl.pallas_call(functools.partial(body, n, (chans, wins, length, groups, p...  52.6 us
    unnamed x3, local copies, waits for them, and re-layouts  1.45 us

profile of v5, /device:TPU:1, one launch (start us, length us, event | category | flops | bytes accessed | tf_op | source)
XLA Modules:
  0.0 54.1 jit_solution(6892200552409116907)
XLA Ops:
  0.0 0.0 copy-start
  0.0 0.7 %copy-done = s32[64]{0:T(128)S(1)} copy-done((s32[64]{0:T(128)S(1)}, s32[64]{0:T(128)}, u32[]{:S(2)}) %copy-start) | copy-done | bytes 280
  0.7 52.6 %shard_map.37 = f32[512,256]{1,0:T(8,128)S(1)} custom-call(s32[64]{0:T(128)S(1)} %copy-done, bf16[16,48,1500]{2,1,0:T(8,128)(2,1)} %traces_hbm.1, bf16[768,1500]{1,0:T(8,128)(2,1)} %constant.2.clone.table_hbm), custom_call_target="tpu_custom_call" | custom-call | tf_op jit(solution)/shard_map/pallas_call | solution.py:325
  53.3 0.8 %copy.5 = f32[2,16,16,256]{3,2,1,0:T(8,128)} copy(f32[2,16,16,256]{3,2,1,0:T(8,128)S(1)} %bitcast.1) | data formatting | bytes 1048576
Async XLA Ops:
  0.0 0.7 %copy-start = (s32[64]{0:T(128)S(1)}, s32[64]{0:T(128)}, u32[]{:S(2)}) copy-start(s32[64]{0:T(128)} %index_ref.1) | copy-start | bytes 772
